TPU v7x, 32 devices: a whole 2x2x4 slice. The times are simulated.
32 devices in a mesh: wide: 16 (over z, y, core), narrow: 2 (over x).
Axes of the slice: x: 2, y: 2, z: 4, core: 2. Of those that a mesh axis runs over, the one named last changes fastest.
Arguments:
- fine_cot: float32 [2, 32, 128, 128], P(None, 'wide', 'narrow'), may hold values from -6 to 6
- obstacle: int32 [2, 32, 128, 128], P(None, 'wide', 'narrow'), may hold values 0 or 1
- sigma: float32 [32, 128, 128], P('wide', 'narrow'), may hold values from 0.2 to 20
Outputs:
- fine_adjoint: float32 [2, 32, 128, 128], P(None, 'wide', 'narrow')
- coarse_adjoint: float32 [16, 2, 16, 64], P('wide', 'narrow')
All inputs are finite; a program needn't handle non-finite values. No bound on the sum of `obstacle` on one device may be relied on, other than what follows from the above.
Results may differ from a plain program's by a relative error of at most 0.00011.
Values sent between devices are 32-bit elements; how exact they have to be, the bound alone decides.
A program may use at most 64 MiB of HBM per device.

v0:
```python
import jax
import jax.numpy as jnp
from jax import lax
from jax.sharding import PartitionSpec as P

SWEEPS = 4
OMEGA = 0.8
COEF_X = 1.0
COEF_Y = 1.0
COEF_Z = 4.0
SHIFT = 0.02


def with_halo(cells, sides, width):
    for axis, dim in sides:
        count = lax.axis_size(axis)
        ends = count - 1
        head = lax.slice_in_dim(cells, 0, width, axis=dim)
        tail = lax.slice_in_dim(cells, cells.shape[dim] - width, cells.shape[dim], axis=dim)
        cells = jnp.concatenate(
            [
                lax.ppermute(tail, axis, [(i, (i + 1) % count) for i in range(ends)]),
                cells,
                lax.ppermute(head, axis, [((i + 1) % count, i) for i in range(ends)]),
            ],
            axis=dim,
        )
    return cells


def sine_table(rows, cols, count):
    product = (rows[:, None] + 1) * (cols[None, :] + 1) % (2 * (count + 1))
    angle = jnp.pi * product.astype(jnp.float32) / (count + 1)
    return jnp.sqrt(2.0 / (count + 1)) * jnp.sin(angle)


def eigen_values(index, count):
    return 2.0 - 2.0 * jnp.cos(jnp.pi * (index + 1).astype(jnp.float32) / (count + 1))


def plane_transform(field):
    count_z = field.shape[2]
    count_y = field.shape[3]
    index_y = jnp.arange(count_y, dtype=jnp.int32)
    index_z = jnp.arange(count_z, dtype=jnp.int32)
    high = lax.Precision.HIGHEST
    field = jnp.einsum(
        "xdzy,yv->xdzv", field, sine_table(index_y, index_y, count_y), precision=high
    )
    return jnp.einsum("xdzv,zw->xdwv", field, sine_table(index_z, index_z, count_z), precision=high)


def plane_denominator(count_z, count_y):
    index_y = jnp.arange(count_y, dtype=jnp.int32)
    index_z = jnp.arange(count_z, dtype=jnp.int32)
    return (
        COEF_Y * eigen_values(index_y, count_y)[None, :]
        + COEF_Z * eigen_values(index_z, count_z)[:, None]
        + SHIFT
    )


def body(fine_cot, obstacle, sigma):
    diag = 6.0 + sigma
    fluid = obstacle.astype(jnp.float32)
    grad = fine_cot
    for sweep in range(SWEEPS):
        weighted = OMEGA * fluid * grad / diag
        padded = with_halo(weighted, (("wide", 1), ("narrow", 2)), 1)
        beside = padded[:, 2:, 1:-1] + padded[:, :-2, 1:-1]
        beside = beside + padded[:, 1:-1, 2:] + padded[:, 1:-1, :-2]
        vertical = jnp.pad(weighted, ((0, 0), (0, 0), (0, 0), (1, 1)))
        beside = beside + vertical[..., 2:] + vertical[..., :-2]
        grad = grad - diag * weighted + beside
    dirs, cells_x, cells_y, cells_z = grad.shape
    coarse = grad.reshape(dirs, cells_x // 2, 2, cells_y // 2, 2, cells_z // 8, 8).sum(
        axis=(2, 4, 6)
    )
    coarse = jnp.transpose(coarse, (1, 0, 3, 2))
    regrouped = lax.all_to_all(coarse, "narrow", split_axis=1, concat_axis=3, tiled=True)
    spectrum = plane_transform(regrouped)
    slabs = spectrum.shape[0]
    total_x = lax.axis_size("wide") * slabs
    own_rows = lax.axis_index("wide") * slabs + jnp.arange(slabs, dtype=jnp.int32)
    plane = plane_denominator(spectrum.shape[2], spectrum.shape[3])
    high = lax.Precision.HIGHEST

    def accumulate(piece):
        columns = jnp.arange(piece.shape[0], dtype=jnp.int32)
        table = sine_table(own_rows, columns, total_x)
        return jnp.einsum("kx,xdwv->kdwv", table, piece, precision=high)

    modes = accumulate(lax.all_gather(spectrum, "wide", axis=0, tiled=True))
    denom = COEF_X * eigen_values(own_rows, total_x)[:, None, None, None] + plane[None, None]
    back = plane_transform(modes / denom)
    coarse_adjoint = accumulate(lax.all_gather(back, "wide", axis=0, tiled=True))
    return (grad, coarse_adjoint)


def solution(mesh):
    placed = (
        P(None, "wide", "narrow", None),
        P(None, "wide", "narrow", None),
        P("wide", "narrow", None),
    )
    return jax.shard_map(
        body,
        mesh=mesh,
        in_specs=placed,
        out_specs=(P(None, "wide", "narrow", None), P("wide", "narrow", None, None)),
        check_vma=False,
    )
```

profile of v0, /device:TPU:0, one launch (start us, length us, event | category | flops | bytes accessed | tf_op | source)
XLA Modules:
  0.0 119.1 jit_solution(6856023964625204232)
XLA Ops:
  0.6 0.9 broadcast_add_fusion
  1.6 0.9 multiply_divide_fusion.3
  2.5 1.3 %collective-permute-start = (f32[2,1,64,128]{3,2,1,0:T(8,128)S(1)}, f32[2,1,64,128]{3,2,1,0:T(8,128)S(1)}, u32[]{:S(2)}, u32[]{:S(2)}) collective-permute-start(f32[2,1,64,128]{3,2,1,0:T(8,128)S(1)} %get-tuple-element.25), channel_id=1, source_target_pairs={{2,0},{4,2},{6,4},{8,6},{10,8},{12,10},{14,12},{16,14},{18,16},{20... | collective-permute-start | bytes 196616 | tf_op jit(solution)/shard_map/ppermute | solution.py:24
  3.8 3.2 %collective-permute-start.1 = (f32[2,1,64,128]{3,2,1,0:T(8,128)S(1)}, f32[2,1,64,128]{3,2,1,0:T(8,128)S(1)}, u32[]{:S(2)}, u32[]{:S(2)}) collective-permute-start(f32[2,1,64,128]{3,2,1,0:T(8,128)S(1)} %get-tuple-element.24), channel_id=1, source_target_pairs={{0,2},{2,4},{4,6},{6,8},{8,10},{10,12},{12,14},{14,16},{16,18},{18... | collective-permute-start | bytes 196616 | tf_op jit(solution)/shard_map/ppermute | solution.py:22
  7.0 0.9 collective-permute-done.1
  7.9 1.3 %collective-permute-start.2 = (f32[2,4,1,128]{3,2,1,0:T(1,128)S(1)}, f32[2,4,1,128]{3,2,1,0:T(1,128)S(1)}, u32[]{:S(2)}, u32[]{:S(2)}) collective-permute-start(f32[2,4,1,128]{3,2,1,0:T(1,128)S(1)} %get-tuple-element.16), channel_id=1, source_target_pairs={{1,0},{3,2},{5,4},{7,6},{9,8},{11,10},{13,12},{15,14},{17,16},{19,... | collective-permute-start | bytes 12296 | tf_op jit(solution)/shard_map/ppermute | solution.py:24
  9.2 4.8 %collective-permute-start.3 = (f32[2,4,1,128]{3,2,1,0:T(1,128)S(1)}, f32[2,4,1,128]{3,2,1,0:T(1,128)S(1)}, u32[]{:S(2)}, u32[]{:S(2)}) collective-permute-start(f32[2,4,1,128]{3,2,1,0:T(1,128)S(1)} %get-tuple-element.17), channel_id=1, source_target_pairs={{0,1},{2,3},{4,5},{6,7},{8,9},{10,11},{12,13},{14,15},{16,17},{18,... | collective-permute-start | bytes 12296 | tf_op jit(solution)/shard_map/ppermute | solution.py:22
  14.0 1.3 %collective-permute-done.3 = f32[2,4,1,128]{3,2,1,0:T(1,128)S(1)} collective-permute-done((f32[2,4,1,128]{3,2,1,0:T(1,128)S(1)}, f32[2,4,1,128]{3,2,1,0:T(1,128)S(1)}, u32[]{:S(2)}, u32[]{:S(2)}) %collective-permute-start.3) | collective-permute-done | bytes 4128 | tf_op jit(solution)/shard_map/ppermute | solution.py:22
  15.5 1.3 %collective-permute-start.4 = (f32[2,1,64,128]{3,2,1,0:T(8,128)S(1)}, f32[2,1,64,128]{3,2,1,0:T(8,128)S(1)}, u32[]{:S(2)}, u32[]{:S(2)}) collective-permute-start(f32[2,1,64,128]{3,2,1,0:T(8,128)S(1)} %get-tuple-element.23), channel_id=1, source_target_pairs={{2,0},{4,2},{6,4},{8,6},{10,8},{12,10},{14,12},{16,14},{18,16},{20... | collective-permute-start | bytes 196616 | tf_op jit(solution)/shard_map/ppermute | solution.py:24
  16.8 4.1 %collective-permute-start.5 = (f32[2,1,64,128]{3,2,1,0:T(8,128)S(1)}, f32[2,1,64,128]{3,2,1,0:T(8,128)S(1)}, u32[]{:S(2)}, u32[]{:S(2)}) collective-permute-start(f32[2,1,64,128]{3,2,1,0:T(8,128)S(1)} %get-tuple-element.22), channel_id=1, source_target_pairs={{0,2},{2,4},{4,6},{6,8},{8,10},{10,12},{12,14},{14,16},{16,18},{18... | collective-permute-start | bytes 196616 | tf_op jit(solution)/shard_map/ppermute | solution.py:22
  21.0 0.9 collective-permute-done.5
  21.8 1.3 %collective-permute-start.6 = (f32[2,4,1,128]{3,2,1,0:T(1,128)S(1)}, f32[2,4,1,128]{3,2,1,0:T(1,128)S(1)}, u32[]{:S(2)}, u32[]{:S(2)}) collective-permute-start(f32[2,4,1,128]{3,2,1,0:T(1,128)S(1)} %get-tuple-element.14), channel_id=1, source_target_pairs={{1,0},{3,2},{5,4},{7,6},{9,8},{11,10},{13,12},{15,14},{17,16},{19,... | collective-permute-start | bytes 12296 | tf_op jit(solution)/shard_map/ppermute | solution.py:24
  23.1 4.5 %collective-permute-start.7 = (f32[2,4,1,128]{3,2,1,0:T(1,128)S(1)}, f32[2,4,1,128]{3,2,1,0:T(1,128)S(1)}, u32[]{:S(2)}, u32[]{:S(2)}) collective-permute-start(f32[2,4,1,128]{3,2,1,0:T(1,128)S(1)} %get-tuple-element.15), channel_id=1, source_target_pairs={{0,1},{2,3},{4,5},{6,7},{8,9},{10,11},{12,13},{14,15},{16,17},{18,... | collective-permute-start | bytes 12296 | tf_op jit(solution)/shard_map/ppermute | solution.py:22
  27.7 1.3 %collective-permute-done.7 = f32[2,4,1,128]{3,2,1,0:T(1,128)S(1)} collective-permute-done((f32[2,4,1,128]{3,2,1,0:T(1,128)S(1)}, f32[2,4,1,128]{3,2,1,0:T(1,128)S(1)}, u32[]{:S(2)}, u32[]{:S(2)}) %collective-permute-start.7) | collective-permute-done | bytes 4128 | tf_op jit(solution)/shard_map/ppermute | solution.py:22
  29.2 1.3 %collective-permute-start.8 = (f32[2,1,64,128]{3,2,1,0:T(8,128)S(1)}, f32[2,1,64,128]{3,2,1,0:T(8,128)S(1)}, u32[]{:S(2)}, u32[]{:S(2)}) collective-permute-start(f32[2,1,64,128]{3,2,1,0:T(8,128)S(1)} %get-tuple-element.21), channel_id=1, source_target_pairs={{2,0},{4,2},{6,4},{8,6},{10,8},{12,10},{14,12},{16,14},{18,16},{20... | collective-permute-start | bytes 196616 | tf_op jit(solution)/shard_map/ppermute | solution.py:24
  30.5 5.8 %collective-permute-start.9 = (f32[2,1,64,128]{3,2,1,0:T(8,128)S(1)}, f32[2,1,64,128]{3,2,1,0:T(8,128)S(1)}, u32[]{:S(2)}, u32[]{:S(2)}) collective-permute-start(f32[2,1,64,128]{3,2,1,0:T(8,128)S(1)} %get-tuple-element.20), channel_id=1, source_target_pairs={{0,2},{2,4},{4,6},{6,8},{8,10},{10,12},{12,14},{14,16},{16,18},{18... | collective-permute-start | bytes 196616 | tf_op jit(solution)/shard_map/ppermute | solution.py:22
  36.3 0.9 collective-permute-done.9
  37.2 1.3 %collective-permute-start.10 = (f32[2,4,1,128]{3,2,1,0:T(1,128)S(1)}, f32[2,4,1,128]{3,2,1,0:T(1,128)S(1)}, u32[]{:S(2)}, u32[]{:S(2)}) collective-permute-start(f32[2,4,1,128]{3,2,1,0:T(1,128)S(1)} %get-tuple-element.12), channel_id=1, source_target_pairs={{1,0},{3,2},{5,4},{7,6},{9,8},{11,10},{13,12},{15,14},{17,16},{19,... | collective-permute-start | bytes 12296 | tf_op jit(solution)/shard_map/ppermute | solution.py:24
  38.5 4.5 %collective-permute-start.11 = (f32[2,4,1,128]{3,2,1,0:T(1,128)S(1)}, f32[2,4,1,128]{3,2,1,0:T(1,128)S(1)}, u32[]{:S(2)}, u32[]{:S(2)}) collective-permute-start(f32[2,4,1,128]{3,2,1,0:T(1,128)S(1)} %get-tuple-element.13), channel_id=1, source_target_pairs={{0,1},{2,3},{4,5},{6,7},{8,9},{10,11},{12,13},{14,15},{16,17},{18,... | collective-permute-start | bytes 12296 | tf_op jit(solution)/shard_map/ppermute | solution.py:22
  43.0 1.3 %collective-permute-done.11 = f32[2,4,1,128]{3,2,1,0:T(1,128)S(1)} collective-permute-done((f32[2,4,1,128]{3,2,1,0:T(1,128)S(1)}, f32[2,4,1,128]{3,2,1,0:T(1,128)S(1)}, u32[]{:S(2)}, u32[]{:S(2)}) %collective-permute-start.11) | collective-permute-done | bytes 4128 | tf_op jit(solution)/shard_map/ppermute | solution.py:22
  44.5 1.3 %collective-permute-start.12 = (f32[2,1,64,128]{3,2,1,0:T(8,128)S(1)}, f32[2,1,64,128]{3,2,1,0:T(8,128)S(1)}, u32[]{:S(2)}, u32[]{:S(2)}) collective-permute-start(f32[2,1,64,128]{3,2,1,0:T(8,128)S(1)} %get-tuple-element.19), channel_id=1, source_target_pairs={{2,0},{4,2},{6,4},{8,6},{10,8},{12,10},{14,12},{16,14},{18,16},{20... | collective-permute-start | bytes 196616 | tf_op jit(solution)/shard_map/ppermute | solution.py:24
  45.8 6.0 %collective-permute-start.13 = (f32[2,1,64,128]{3,2,1,0:T(8,128)S(1)}, f32[2,1,64,128]{3,2,1,0:T(8,128)S(1)}, u32[]{:S(2)}, u32[]{:S(2)}) collective-permute-start(f32[2,1,64,128]{3,2,1,0:T(8,128)S(1)} %get-tuple-element.18), channel_id=1, source_target_pairs={{0,2},{2,4},{4,6},{6,8},{8,10},{10,12},{12,14},{14,16},{16,18},{18... | collective-permute-start | bytes 196616 | tf_op jit(solution)/shard_map/ppermute | solution.py:22
  51.9 0.9 collective-permute-done.13
  52.7 1.3 %collective-permute-start.14 = (f32[2,4,1,128]{3,2,1,0:T(1,128)S(1)}, f32[2,4,1,128]{3,2,1,0:T(1,128)S(1)}, u32[]{:S(2)}, u32[]{:S(2)}) collective-permute-start(f32[2,4,1,128]{3,2,1,0:T(1,128)S(1)} %get-tuple-element.10), channel_id=1, source_target_pairs={{1,0},{3,2},{5,4},{7,6},{9,8},{11,10},{13,12},{15,14},{17,16},{19,... | collective-permute-start | bytes 12296 | tf_op jit(solution)/shard_map/ppermute | solution.py:24
  54.0 4.5 %collective-permute-start.15 = (f32[2,4,1,128]{3,2,1,0:T(1,128)S(1)}, f32[2,4,1,128]{3,2,1,0:T(1,128)S(1)}, u32[]{:S(2)}, u32[]{:S(2)}) collective-permute-start(f32[2,4,1,128]{3,2,1,0:T(1,128)S(1)} %get-tuple-element.11), channel_id=1, source_target_pairs={{0,1},{2,3},{4,5},{6,7},{8,9},{10,11},{12,13},{14,15},{16,17},{18,... | collective-permute-start | bytes 12296 | tf_op jit(solution)/shard_map/ppermute | solution.py:22
  58.6 1.3 %collective-permute-done.15 = f32[2,4,1,128]{3,2,1,0:T(1,128)S(1)} collective-permute-done((f32[2,4,1,128]{3,2,1,0:T(1,128)S(1)}, f32[2,4,1,128]{3,2,1,0:T(1,128)S(1)}, u32[]{:S(2)}, u32[]{:S(2)}) %collective-permute-start.15) | collective-permute-done | bytes 4128 | tf_op jit(solution)/shard_map/ppermute | solution.py:22
  59.9 0.8 fusion.118
  62.2 3.5 %all-to-all-start = ((f32[2,1,512]{2,1,0:T(1,128)}), f32[2,1,512]{2,1,0:T(1,128)S(1)}, u32[]{:S(2)}, u32[]{:S(2)}) async-start(f32[2,1,512]{2,1,0:T(1,128)} %reshape.164), calls=%async_computation | async-start | bytes 8192 | tf_op jit(solution)/shard_map/all_to_all | solution.py:80
  65.9 3.7 %all-to-all-done = f32[2,1,512]{2,1,0:T(1,128)S(1)} async-done(((f32[2,1,512]{2,1,0:T(1,128)}), f32[2,1,512]{2,1,0:T(1,128)S(1)}, u32[]{:S(2)}, u32[]{:S(2)}) %all-to-all-start) | async-done | bytes 4128 | tf_op jit(solution)/shard_map/all_to_all | solution.py:80
  71.6 27.9 %all-gather = f32[256,64]{1,0:T(8,128)S(1)} all-gather(f32[16,64]{1,0:T(8,128)S(1)} %fusion.64), channel_id=2, replica_groups=mesh['wide'=16,'narrow'=2] {'wide'}, dimensions={0}, use_global_device_ids=true | all-gather | bytes 69632 | tf_op jit(solution)/shard_map/all_gather | solution.py:93
  100.4 17.8 %all-gather.1 = f32[256,64]{1,0:T(8,128)S(1)} all-gather(f32[16,64]{1,0:T(8,128)S(1)} %fusion.62), channel_id=3, replica_groups=mesh['wide'=16,'narrow'=2] {'wide'}, dimensions={0}, use_global_device_ids=true | all-gather | bytes 69632 | tf_op jit(solution)/shard_map/all_gather | solution.py:96
  118.2 0.9 fusion.24
  (42 shorter events, 5.2 us)
Async XLA Ops:
  0.6 0.9 copy-start
  2.5 4.5 %collective-permute-start = (f32[2,1,64,128]{3,2,1,0:T(8,128)S(1)}, f32[2,1,64,128]{3,2,1,0:T(8,128)S(1)}, u32[]{:S(2)}, u32[]{:S(2)}) collective-permute-start(f32[2,1,64,128]{3,2,1,0:T(8,128)S(1)} %get-tuple-element.25), channel_id=1, source_target_pairs={{2,0},{4,2},{6,4},{8,6},{10,8},{12,10},{14,12},{16,14},{18,16},{20... | collective-permute-start | bytes 196616 | tf_op jit(solution)/shard_map/ppermute | solution.py:24
  3.8 11.5 %copy-start.1 = (f32[2,2,64,128]{3,2,1,0:T(8,128)S(1)}, f32[2,2,64,128]{3,2,1,0:T(8,128)}, u32[]{:S(2)}) copy-start(f32[2,2,64,128]{3,2,1,0:T(8,128)} %param.3) | copy-start | bytes 393220
  3.8 4.1 %collective-permute-start.1 = (f32[2,1,64,128]{3,2,1,0:T(8,128)S(1)}, f32[2,1,64,128]{3,2,1,0:T(8,128)S(1)}, u32[]{:S(2)}, u32[]{:S(2)}) collective-permute-start(f32[2,1,64,128]{3,2,1,0:T(8,128)S(1)} %get-tuple-element.24), channel_id=1, source_target_pairs={{0,2},{2,4},{4,6},{6,8},{8,10},{10,12},{12,14},{14,16},{16,18},{18... | collective-permute-start | bytes 196616 | tf_op jit(solution)/shard_map/ppermute | solution.py:22
  7.9 6.1 %collective-permute-start.2 = (f32[2,4,1,128]{3,2,1,0:T(1,128)S(1)}, f32[2,4,1,128]{3,2,1,0:T(1,128)S(1)}, u32[]{:S(2)}, u32[]{:S(2)}) collective-permute-start(f32[2,4,1,128]{3,2,1,0:T(1,128)S(1)} %get-tuple-element.16), channel_id=1, source_target_pairs={{1,0},{3,2},{5,4},{7,6},{9,8},{11,10},{13,12},{15,14},{17,16},{19,... | collective-permute-start | bytes 12296 | tf_op jit(solution)/shard_map/ppermute | solution.py:24
  9.2 6.2 %collective-permute-start.3 = (f32[2,4,1,128]{3,2,1,0:T(1,128)S(1)}, f32[2,4,1,128]{3,2,1,0:T(1,128)S(1)}, u32[]{:S(2)}, u32[]{:S(2)}) collective-permute-start(f32[2,4,1,128]{3,2,1,0:T(1,128)S(1)} %get-tuple-element.17), channel_id=1, source_target_pairs={{0,1},{2,3},{4,5},{6,7},{8,9},{10,11},{12,13},{14,15},{16,17},{18,... | collective-permute-start | bytes 12296 | tf_op jit(solution)/shard_map/ppermute | solution.py:22
  15.5 5.4 %collective-permute-start.4 = (f32[2,1,64,128]{3,2,1,0:T(8,128)S(1)}, f32[2,1,64,128]{3,2,1,0:T(8,128)S(1)}, u32[]{:S(2)}, u32[]{:S(2)}) collective-permute-start(f32[2,1,64,128]{3,2,1,0:T(8,128)S(1)} %get-tuple-element.23), channel_id=1, source_target_pairs={{2,0},{4,2},{6,4},{8,6},{10,8},{12,10},{14,12},{16,14},{18,16},{20... | collective-permute-start | bytes 196616 | tf_op jit(solution)/shard_map/ppermute | solution.py:24
  16.8 5.0 %collective-permute-start.5 = (f32[2,1,64,128]{3,2,1,0:T(8,128)S(1)}, f32[2,1,64,128]{3,2,1,0:T(8,128)S(1)}, u32[]{:S(2)}, u32[]{:S(2)}) collective-permute-start(f32[2,1,64,128]{3,2,1,0:T(8,128)S(1)} %get-tuple-element.22), channel_id=1, source_target_pairs={{0,2},{2,4},{4,6},{6,8},{8,10},{10,12},{12,14},{14,16},{16,18},{18... | collective-permute-start | bytes 196616 | tf_op jit(solution)/shard_map/ppermute | solution.py:22
  21.8 5.8 %collective-permute-start.6 = (f32[2,4,1,128]{3,2,1,0:T(1,128)S(1)}, f32[2,4,1,128]{3,2,1,0:T(1,128)S(1)}, u32[]{:S(2)}, u32[]{:S(2)}) collective-permute-start(f32[2,4,1,128]{3,2,1,0:T(1,128)S(1)} %get-tuple-element.14), channel_id=1, source_target_pairs={{1,0},{3,2},{5,4},{7,6},{9,8},{11,10},{13,12},{15,14},{17,16},{19,... | collective-permute-start | bytes 12296 | tf_op jit(solution)/shard_map/ppermute | solution.py:24
  23.1 5.9 %collective-permute-start.7 = (f32[2,4,1,128]{3,2,1,0:T(1,128)S(1)}, f32[2,4,1,128]{3,2,1,0:T(1,128)S(1)}, u32[]{:S(2)}, u32[]{:S(2)}) collective-permute-start(f32[2,4,1,128]{3,2,1,0:T(1,128)S(1)} %get-tuple-element.15), channel_id=1, source_target_pairs={{0,1},{2,3},{4,5},{6,7},{8,9},{10,11},{12,13},{14,15},{16,17},{18,... | collective-permute-start | bytes 12296 | tf_op jit(solution)/shard_map/ppermute | solution.py:22
  29.2 7.1 %collective-permute-start.8 = (f32[2,1,64,128]{3,2,1,0:T(8,128)S(1)}, f32[2,1,64,128]{3,2,1,0:T(8,128)S(1)}, u32[]{:S(2)}, u32[]{:S(2)}) collective-permute-start(f32[2,1,64,128]{3,2,1,0:T(8,128)S(1)} %get-tuple-element.21), channel_id=1, source_target_pairs={{2,0},{4,2},{6,4},{8,6},{10,8},{12,10},{14,12},{16,14},{18,16},{20... | collective-permute-start | bytes 196616 | tf_op jit(solution)/shard_map/ppermute | solution.py:24
  30.5 6.7 %collective-permute-start.9 = (f32[2,1,64,128]{3,2,1,0:T(8,128)S(1)}, f32[2,1,64,128]{3,2,1,0:T(8,128)S(1)}, u32[]{:S(2)}, u32[]{:S(2)}) collective-permute-start(f32[2,1,64,128]{3,2,1,0:T(8,128)S(1)} %get-tuple-element.20), channel_id=1, source_target_pairs={{0,2},{2,4},{4,6},{6,8},{8,10},{10,12},{12,14},{14,16},{16,18},{18... | collective-permute-start | bytes 196616 | tf_op jit(solution)/shard_map/ppermute | solution.py:22
  37.2 5.9 %collective-permute-start.10 = (f32[2,4,1,128]{3,2,1,0:T(1,128)S(1)}, f32[2,4,1,128]{3,2,1,0:T(1,128)S(1)}, u32[]{:S(2)}, u32[]{:S(2)}) collective-permute-start(f32[2,4,1,128]{3,2,1,0:T(1,128)S(1)} %get-tuple-element.12), channel_id=1, source_target_pairs={{1,0},{3,2},{5,4},{7,6},{9,8},{11,10},{13,12},{15,14},{17,16},{19,... | collective-permute-start | bytes 12296 | tf_op jit(solution)/shard_map/ppermute | solution.py:24
  38.5 5.9 %collective-permute-start.11 = (f32[2,4,1,128]{3,2,1,0:T(1,128)S(1)}, f32[2,4,1,128]{3,2,1,0:T(1,128)S(1)}, u32[]{:S(2)}, u32[]{:S(2)}) collective-permute-start(f32[2,4,1,128]{3,2,1,0:T(1,128)S(1)} %get-tuple-element.13), channel_id=1, source_target_pairs={{0,1},{2,3},{4,5},{6,7},{8,9},{10,11},{12,13},{14,15},{16,17},{18,... | collective-permute-start | bytes 12296 | tf_op jit(solution)/shard_map/ppermute | solution.py:22
  44.5 7.4 %collective-permute-start.12 = (f32[2,1,64,128]{3,2,1,0:T(8,128)S(1)}, f32[2,1,64,128]{3,2,1,0:T(8,128)S(1)}, u32[]{:S(2)}, u32[]{:S(2)}) collective-permute-start(f32[2,1,64,128]{3,2,1,0:T(8,128)S(1)} %get-tuple-element.19), channel_id=1, source_target_pairs={{2,0},{4,2},{6,4},{8,6},{10,8},{12,10},{14,12},{16,14},{18,16},{20... | collective-permute-start | bytes 196616 | tf_op jit(solution)/shard_map/ppermute | solution.py:24
  45.8 6.9 %collective-permute-start.13 = (f32[2,1,64,128]{3,2,1,0:T(8,128)S(1)}, f32[2,1,64,128]{3,2,1,0:T(8,128)S(1)}, u32[]{:S(2)}, u32[]{:S(2)}) collective-permute-start(f32[2,1,64,128]{3,2,1,0:T(8,128)S(1)} %get-tuple-element.18), channel_id=1, source_target_pairs={{0,2},{2,4},{4,6},{6,8},{8,10},{10,12},{12,14},{14,16},{16,18},{18... | collective-permute-start | bytes 196616 | tf_op jit(solution)/shard_map/ppermute | solution.py:22
  52.7 5.9 %collective-permute-start.14 = (f32[2,4,1,128]{3,2,1,0:T(1,128)S(1)}, f32[2,4,1,128]{3,2,1,0:T(1,128)S(1)}, u32[]{:S(2)}, u32[]{:S(2)}) collective-permute-start(f32[2,4,1,128]{3,2,1,0:T(1,128)S(1)} %get-tuple-element.10), channel_id=1, source_target_pairs={{1,0},{3,2},{5,4},{7,6},{9,8},{11,10},{13,12},{15,14},{17,16},{19,... | collective-permute-start | bytes 12296 | tf_op jit(solution)/shard_map/ppermute | solution.py:24
  54.0 5.9 %collective-permute-start.15 = (f32[2,4,1,128]{3,2,1,0:T(1,128)S(1)}, f32[2,4,1,128]{3,2,1,0:T(1,128)S(1)}, u32[]{:S(2)}, u32[]{:S(2)}) collective-permute-start(f32[2,4,1,128]{3,2,1,0:T(1,128)S(1)} %get-tuple-element.11), channel_id=1, source_target_pairs={{0,1},{2,3},{4,5},{6,7},{8,9},{10,11},{12,13},{14,15},{16,17},{18,... | collective-permute-start | bytes 12296 | tf_op jit(solution)/shard_map/ppermute | solution.py:22
  62.2 7.3 %all-to-all-start = ((f32[2,1,512]{2,1,0:T(1,128)}), f32[2,1,512]{2,1,0:T(1,128)S(1)}, u32[]{:S(2)}, u32[]{:S(2)}) async-start(f32[2,1,512]{2,1,0:T(1,128)} %reshape.164), calls=%async_computation | async-start | bytes 8192 | tf_op jit(solution)/shard_map/all_to_all | solution.py:80
where the time goes:
time: 120 us; the launch traced here: 119 us
  starting transfers between devices  51.4 us (43%)
  blocking collectives  45.7 us (38%)
  waiting for transfers between devices  12.3 us (10%)
  other arithmetic  4.09 us (3%)
  matrix products  2.44 us (2%)
  local copies, waits for them, and re-layouts  2.1 us (2%)
    ppermute x8, starting transfers between devices, with_halo(): lax.ppermute(tail, axis, [(i, (i + 1) % count) for i in range(ends)])  37.6 us
    all_gather x1, blocking collectives, body(): modes = accumulate(lax.all_gather(spectrum, 'wide', axis=0, tiled=True))  27.9 us
    all_gather x1, blocking collectives, body(): lax.all_gather(back, 'wide', axis=0, tiled=True)  17.8 us
    ppermute x8, starting transfers between devices, with_halo(): lax.ppermute(head, axis, [((i + 1) % count, i) for i in range(ends)])  10.3 us
    ppermute x8, waiting for transfers between devices, with_halo(): lax.ppermute(tail, axis, [(i, (i + 1) % count) for i in range(ends)])  8.62 us
    all_to_all x1, waiting for transfers between devices, body(): lax.all_to_all(coarse, 'narrow', split_axis=1, concat_axis=3, tiled=True)  3.66 us
    all_to_all x1, starting transfers between devices, body(): lax.all_to_all(coarse, 'narrow', split_axis=1, concat_axis=3, tiled=True)  3.55 us
  transfers between devices with their start and end apart: 17, of which 9 were waited for; matrix products, arithmetic and copies ran while one was open for 0% of the time, Pallas kernels for 0%

commit v1 on v0

--- a/solution.py
+++ b/solution.py
@@ -77,7 +77,12 @@
         axis=(2, 4, 6)
     )
     coarse = jnp.transpose(coarse, (1, 0, 3, 2))
-    regrouped = lax.all_to_all(coarse, "narrow", split_axis=1, concat_axis=3, tiled=True)
+    regrouped = jnp.concatenate(
+        lax.all_to_all(
+            jnp.stack(jnp.split(coarse, lax.axis_size("narrow"), axis=1)), "narrow", 0, 0
+        ),
+        axis=3,
+    )
     spectrum = plane_transform(regrouped)
     slabs = spectrum.shape[0]
     total_x = lax.axis_size("wide") * slabs

time: 120 us -> 120 us (level)
  no operation moved by 1% of the time
where the time goes in v1:
time: 120 us; the launch traced here: 119 us
  starting transfers between devices  51.4 us (43%)
  blocking collectives  45.7 us (38%)
  waiting for transfers between devices  12.3 us (10%)
  other arithmetic  4.1 us (3%)
  matrix products  2.44 us (2%)
  local copies, waits for them, and re-layouts  2.1 us (2%)
    ppermute x8, starting transfers between devices, with_halo(): lax.ppermute(tail, axis, [(i, (i + 1) % count) for i in range(ends)])  37.6 us
    all_gather x1, blocking collectives, body(): modes = accumulate(lax.all_gather(spectrum, 'wide', axis=0, tiled=True))  27.9 us
    all_gather x1, blocking collectives, body(): lax.all_gather(back, 'wide', axis=0, tiled=True)  17.8 us
    ppermute x8, starting transfers between devices, with_halo(): lax.ppermute(head, axis, [((i + 1) % count, i) for i in range(ends)])  10.3 us
    ppermute x8, waiting for transfers between devices, with_halo(): lax.ppermute(tail, axis, [(i, (i + 1) % count) for i in range(ends)])  8.62 us
    all_to_all x1, waiting for transfers between devices, body(): lax.all_to_all(jnp.stack(jnp.split(coarse, lax.axis_size('narrow'), axis=...  3.66 us
    all_to_all x1, starting transfers between devices, body(): lax.all_to_all(jnp.stack(jnp.split(coarse, lax.axis_size('narrow'), axis=...  3.55 us
  transfers between devices with their start and end apart: 17, of which 9 were waited for; matrix products, arithmetic and copies ran while one was open for 0% of the time, Pallas kernels for 0%

profile of v1, /device:TPU:0, one launch (start us, length us, event | category | flops | bytes accessed | tf_op | source)
XLA Modules:
  0.0 119.1 jit_solution(4796031338043887256)
XLA Ops:
  0.6 0.9 broadcast_add_fusion
  1.6 0.9 multiply_divide_fusion.3
  2.5 1.3 %collective-permute-start = (f32[2,1,64,128]{3,2,1,0:T(8,128)S(1)}, f32[2,1,64,128]{3,2,1,0:T(8,128)S(1)}, u32[]{:S(2)}, u32[]{:S(2)}) collective-permute-start(f32[2,1,64,128]{3,2,1,0:T(8,128)S(1)} %get-tuple-element.25), channel_id=1, source_target_pairs={{2,0},{4,2},{6,4},{8,6},{10,8},{12,10},{14,12},{16,14},{18,16},{20... | collective-permute-start | bytes 196616 | tf_op jit(solution)/shard_map/ppermute | solution.py:24
  3.8 3.2 %collective-permute-start.1 = (f32[2,1,64,128]{3,2,1,0:T(8,128)S(1)}, f32[2,1,64,128]{3,2,1,0:T(8,128)S(1)}, u32[]{:S(2)}, u32[]{:S(2)}) collective-permute-start(f32[2,1,64,128]{3,2,1,0:T(8,128)S(1)} %get-tuple-element.24), channel_id=1, source_target_pairs={{0,2},{2,4},{4,6},{6,8},{8,10},{10,12},{12,14},{14,16},{16,18},{18... | collective-permute-start | bytes 196616 | tf_op jit(solution)/shard_map/ppermute | solution.py:22
  7.0 0.9 collective-permute-done.1
  7.9 1.3 %collective-permute-start.2 = (f32[2,4,1,128]{3,2,1,0:T(1,128)S(1)}, f32[2,4,1,128]{3,2,1,0:T(1,128)S(1)}, u32[]{:S(2)}, u32[]{:S(2)}) collective-permute-start(f32[2,4,1,128]{3,2,1,0:T(1,128)S(1)} %get-tuple-element.16), channel_id=1, source_target_pairs={{1,0},{3,2},{5,4},{7,6},{9,8},{11,10},{13,12},{15,14},{17,16},{19,... | collective-permute-start | bytes 12296 | tf_op jit(solution)/shard_map/ppermute | solution.py:24
  9.2 4.8 %collective-permute-start.3 = (f32[2,4,1,128]{3,2,1,0:T(1,128)S(1)}, f32[2,4,1,128]{3,2,1,0:T(1,128)S(1)}, u32[]{:S(2)}, u32[]{:S(2)}) collective-permute-start(f32[2,4,1,128]{3,2,1,0:T(1,128)S(1)} %get-tuple-element.17), channel_id=1, source_target_pairs={{0,1},{2,3},{4,5},{6,7},{8,9},{10,11},{12,13},{14,15},{16,17},{18,... | collective-permute-start | bytes 12296 | tf_op jit(solution)/shard_map/ppermute | solution.py:22
  14.0 1.3 %collective-permute-done.3 = f32[2,4,1,128]{3,2,1,0:T(1,128)S(1)} collective-permute-done((f32[2,4,1,128]{3,2,1,0:T(1,128)S(1)}, f32[2,4,1,128]{3,2,1,0:T(1,128)S(1)}, u32[]{:S(2)}, u32[]{:S(2)}) %collective-permute-start.3) | collective-permute-done | bytes 4128 | tf_op jit(solution)/shard_map/ppermute | solution.py:22
  15.5 1.3 %collective-permute-start.4 = (f32[2,1,64,128]{3,2,1,0:T(8,128)S(1)}, f32[2,1,64,128]{3,2,1,0:T(8,128)S(1)}, u32[]{:S(2)}, u32[]{:S(2)}) collective-permute-start(f32[2,1,64,128]{3,2,1,0:T(8,128)S(1)} %get-tuple-element.23), channel_id=1, source_target_pairs={{2,0},{4,2},{6,4},{8,6},{10,8},{12,10},{14,12},{16,14},{18,16},{20... | collective-permute-start | bytes 196616 | tf_op jit(solution)/shard_map/ppermute | solution.py:24
  16.8 4.1 %collective-permute-start.5 = (f32[2,1,64,128]{3,2,1,0:T(8,128)S(1)}, f32[2,1,64,128]{3,2,1,0:T(8,128)S(1)}, u32[]{:S(2)}, u32[]{:S(2)}) collective-permute-start(f32[2,1,64,128]{3,2,1,0:T(8,128)S(1)} %get-tuple-element.22), channel_id=1, source_target_pairs={{0,2},{2,4},{4,6},{6,8},{8,10},{10,12},{12,14},{14,16},{16,18},{18... | collective-permute-start | bytes 196616 | tf_op jit(solution)/shard_map/ppermute | solution.py:22
  21.0 0.9 collective-permute-done.5
  21.8 1.3 %collective-permute-start.6 = (f32[2,4,1,128]{3,2,1,0:T(1,128)S(1)}, f32[2,4,1,128]{3,2,1,0:T(1,128)S(1)}, u32[]{:S(2)}, u32[]{:S(2)}) collective-permute-start(f32[2,4,1,128]{3,2,1,0:T(1,128)S(1)} %get-tuple-element.14), channel_id=1, source_target_pairs={{1,0},{3,2},{5,4},{7,6},{9,8},{11,10},{13,12},{15,14},{17,16},{19,... | collective-permute-start | bytes 12296 | tf_op jit(solution)/shard_map/ppermute | solution.py:24
  23.1 4.5 %collective-permute-start.7 = (f32[2,4,1,128]{3,2,1,0:T(1,128)S(1)}, f32[2,4,1,128]{3,2,1,0:T(1,128)S(1)}, u32[]{:S(2)}, u32[]{:S(2)}) collective-permute-start(f32[2,4,1,128]{3,2,1,0:T(1,128)S(1)} %get-tuple-element.15), channel_id=1, source_target_pairs={{0,1},{2,3},{4,5},{6,7},{8,9},{10,11},{12,13},{14,15},{16,17},{18,... | collective-permute-start | bytes 12296 | tf_op jit(solution)/shard_map/ppermute | solution.py:22
  27.7 1.3 %collective-permute-done.7 = f32[2,4,1,128]{3,2,1,0:T(1,128)S(1)} collective-permute-done((f32[2,4,1,128]{3,2,1,0:T(1,128)S(1)}, f32[2,4,1,128]{3,2,1,0:T(1,128)S(1)}, u32[]{:S(2)}, u32[]{:S(2)}) %collective-permute-start.7) | collective-permute-done | bytes 4128 | tf_op jit(solution)/shard_map/ppermute | solution.py:22
  29.2 1.3 %collective-permute-start.8 = (f32[2,1,64,128]{3,2,1,0:T(8,128)S(1)}, f32[2,1,64,128]{3,2,1,0:T(8,128)S(1)}, u32[]{:S(2)}, u32[]{:S(2)}) collective-permute-start(f32[2,1,64,128]{3,2,1,0:T(8,128)S(1)} %get-tuple-element.21), channel_id=1, source_target_pairs={{2,0},{4,2},{6,4},{8,6},{10,8},{12,10},{14,12},{16,14},{18,16},{20... | collective-permute-start | bytes 196616 | tf_op jit(solution)/shard_map/ppermute | solution.py:24
  30.5 5.8 %collective-permute-start.9 = (f32[2,1,64,128]{3,2,1,0:T(8,128)S(1)}, f32[2,1,64,128]{3,2,1,0:T(8,128)S(1)}, u32[]{:S(2)}, u32[]{:S(2)}) collective-permute-start(f32[2,1,64,128]{3,2,1,0:T(8,128)S(1)} %get-tuple-element.20), channel_id=1, source_target_pairs={{0,2},{2,4},{4,6},{6,8},{8,10},{10,12},{12,14},{14,16},{16,18},{18... | collective-permute-start | bytes 196616 | tf_op jit(solution)/shard_map/ppermute | solution.py:22
  36.3 0.9 collective-permute-done.9
  37.2 1.3 %collective-permute-start.10 = (f32[2,4,1,128]{3,2,1,0:T(1,128)S(1)}, f32[2,4,1,128]{3,2,1,0:T(1,128)S(1)}, u32[]{:S(2)}, u32[]{:S(2)}) collective-permute-start(f32[2,4,1,128]{3,2,1,0:T(1,128)S(1)} %get-tuple-element.12), channel_id=1, source_target_pairs={{1,0},{3,2},{5,4},{7,6},{9,8},{11,10},{13,12},{15,14},{17,16},{19,... | collective-permute-start | bytes 12296 | tf_op jit(solution)/shard_map/ppermute | solution.py:24
  38.5 4.5 %collective-permute-start.11 = (f32[2,4,1,128]{3,2,1,0:T(1,128)S(1)}, f32[2,4,1,128]{3,2,1,0:T(1,128)S(1)}, u32[]{:S(2)}, u32[]{:S(2)}) collective-permute-start(f32[2,4,1,128]{3,2,1,0:T(1,128)S(1)} %get-tuple-element.13), channel_id=1, source_target_pairs={{0,1},{2,3},{4,5},{6,7},{8,9},{10,11},{12,13},{14,15},{16,17},{18,... | collective-permute-start | bytes 12296 | tf_op jit(solution)/shard_map/ppermute | solution.py:22
  43.0 1.3 %collective-permute-done.11 = f32[2,4,1,128]{3,2,1,0:T(1,128)S(1)} collective-permute-done((f32[2,4,1,128]{3,2,1,0:T(1,128)S(1)}, f32[2,4,1,128]{3,2,1,0:T(1,128)S(1)}, u32[]{:S(2)}, u32[]{:S(2)}) %collective-permute-start.11) | collective-permute-done | bytes 4128 | tf_op jit(solution)/shard_map/ppermute | solution.py:22
  44.5 1.3 %collective-permute-start.12 = (f32[2,1,64,128]{3,2,1,0:T(8,128)S(1)}, f32[2,1,64,128]{3,2,1,0:T(8,128)S(1)}, u32[]{:S(2)}, u32[]{:S(2)}) collective-permute-start(f32[2,1,64,128]{3,2,1,0:T(8,128)S(1)} %get-tuple-element.19), channel_id=1, source_target_pairs={{2,0},{4,2},{6,4},{8,6},{10,8},{12,10},{14,12},{16,14},{18,16},{20... | collective-permute-start | bytes 196616 | tf_op jit(solution)/shard_map/ppermute | solution.py:24
  45.8 6.0 %collective-permute-start.13 = (f32[2,1,64,128]{3,2,1,0:T(8,128)S(1)}, f32[2,1,64,128]{3,2,1,0:T(8,128)S(1)}, u32[]{:S(2)}, u32[]{:S(2)}) collective-permute-start(f32[2,1,64,128]{3,2,1,0:T(8,128)S(1)} %get-tuple-element.18), channel_id=1, source_target_pairs={{0,2},{2,4},{4,6},{6,8},{8,10},{10,12},{12,14},{14,16},{16,18},{18... | collective-permute-start | bytes 196616 | tf_op jit(solution)/shard_map/ppermute | solution.py:22
  51.9 0.9 collective-permute-done.13
  52.7 1.3 %collective-permute-start.14 = (f32[2,4,1,128]{3,2,1,0:T(1,128)S(1)}, f32[2,4,1,128]{3,2,1,0:T(1,128)S(1)}, u32[]{:S(2)}, u32[]{:S(2)}) collective-permute-start(f32[2,4,1,128]{3,2,1,0:T(1,128)S(1)} %get-tuple-element.10), channel_id=1, source_target_pairs={{1,0},{3,2},{5,4},{7,6},{9,8},{11,10},{13,12},{15,14},{17,16},{19,... | collective-permute-start | bytes 12296 | tf_op jit(solution)/shard_map/ppermute | solution.py:24
  54.0 4.5 %collective-permute-start.15 = (f32[2,4,1,128]{3,2,1,0:T(1,128)S(1)}, f32[2,4,1,128]{3,2,1,0:T(1,128)S(1)}, u32[]{:S(2)}, u32[]{:S(2)}) collective-permute-start(f32[2,4,1,128]{3,2,1,0:T(1,128)S(1)} %get-tuple-element.11), channel_id=1, source_target_pairs={{0,1},{2,3},{4,5},{6,7},{8,9},{10,11},{12,13},{14,15},{16,17},{18,... | collective-permute-start | bytes 12296 | tf_op jit(solution)/shard_map/ppermute | solution.py:22
  58.6 1.3 %collective-permute-done.15 = f32[2,4,1,128]{3,2,1,0:T(1,128)S(1)} collective-permute-done((f32[2,4,1,128]{3,2,1,0:T(1,128)S(1)}, f32[2,4,1,128]{3,2,1,0:T(1,128)S(1)}, u32[]{:S(2)}, u32[]{:S(2)}) %collective-permute-start.15) | collective-permute-done | bytes 4128 | tf_op jit(solution)/shard_map/ppermute | solution.py:22
  59.9 0.8 fusion.118
  62.3 3.5 %all-to-all-start = ((f32[2,1,512]{2,1,0:T(1,128)}), f32[2,1,512]{2,1,0:T(1,128)S(1)}, u32[]{:S(2)}, u32[]{:S(2)}) async-start(f32[2,1,512]{2,1,0:T(1,128)} %reshape.169), calls=%async_computation | async-start | bytes 8192 | tf_op jit(solution)/shard_map/all_to_all | solution.py:81
  65.9 3.7 %all-to-all-done = f32[2,1,512]{2,1,0:T(1,128)S(1)} async-done(((f32[2,1,512]{2,1,0:T(1,128)}), f32[2,1,512]{2,1,0:T(1,128)S(1)}, u32[]{:S(2)}, u32[]{:S(2)}) %all-to-all-start) | async-done | bytes 4128 | tf_op jit(solution)/shard_map/all_to_all | solution.py:81
  71.6 27.9 %all-gather = f32[256,64]{1,0:T(8,128)S(1)} all-gather(f32[16,64]{1,0:T(8,128)S(1)} %fusion.64), channel_id=2, replica_groups=mesh['wide'=16,'narrow'=2] {'wide'}, dimensions={0}, use_global_device_ids=true | all-gather | bytes 69632 | tf_op jit(solution)/shard_map/all_gather | solution.py:98
  100.4 17.8 %all-gather.1 = f32[256,64]{1,0:T(8,128)S(1)} all-gather(f32[16,64]{1,0:T(8,128)S(1)} %fusion.62), channel_id=3, replica_groups=mesh['wide'=16,'narrow'=2] {'wide'}, dimensions={0}, use_global_device_ids=true | all-gather | bytes 69632 | tf_op jit(solution)/shard_map/all_gather | solution.py:101
  118.2 0.9 fusion.24
  (43 shorter events, 5.2 us)
Async XLA Ops:
  0.6 0.9 copy-start
  2.5 4.5 %collective-permute-start = (f32[2,1,64,128]{3,2,1,0:T(8,128)S(1)}, f32[2,1,64,128]{3,2,1,0:T(8,128)S(1)}, u32[]{:S(2)}, u32[]{:S(2)}) collective-permute-start(f32[2,1,64,128]{3,2,1,0:T(8,128)S(1)} %get-tuple-element.25), channel_id=1, source_target_pairs={{2,0},{4,2},{6,4},{8,6},{10,8},{12,10},{14,12},{16,14},{18,16},{20... | collective-permute-start | bytes 196616 | tf_op jit(solution)/shard_map/ppermute | solution.py:24
  3.8 11.5 %copy-start.1 = (f32[2,2,64,128]{3,2,1,0:T(8,128)S(1)}, f32[2,2,64,128]{3,2,1,0:T(8,128)}, u32[]{:S(2)}) copy-start(f32[2,2,64,128]{3,2,1,0:T(8,128)} %param.3) | copy-start | bytes 393220
  3.8 4.1 %collective-permute-start.1 = (f32[2,1,64,128]{3,2,1,0:T(8,128)S(1)}, f32[2,1,64,128]{3,2,1,0:T(8,128)S(1)}, u32[]{:S(2)}, u32[]{:S(2)}) collective-permute-start(f32[2,1,64,128]{3,2,1,0:T(8,128)S(1)} %get-tuple-element.24), channel_id=1, source_target_pairs={{0,2},{2,4},{4,6},{6,8},{8,10},{10,12},{12,14},{14,16},{16,18},{18... | collective-permute-start | bytes 196616 | tf_op jit(solution)/shard_map/ppermute | solution.py:22
  7.9 6.1 %collective-permute-start.2 = (f32[2,4,1,128]{3,2,1,0:T(1,128)S(1)}, f32[2,4,1,128]{3,2,1,0:T(1,128)S(1)}, u32[]{:S(2)}, u32[]{:S(2)}) collective-permute-start(f32[2,4,1,128]{3,2,1,0:T(1,128)S(1)} %get-tuple-element.16), channel_id=1, source_target_pairs={{1,0},{3,2},{5,4},{7,6},{9,8},{11,10},{13,12},{15,14},{17,16},{19,... | collective-permute-start | bytes 12296 | tf_op jit(solution)/shard_map/ppermute | solution.py:24
  9.2 6.2 %collective-permute-start.3 = (f32[2,4,1,128]{3,2,1,0:T(1,128)S(1)}, f32[2,4,1,128]{3,2,1,0:T(1,128)S(1)}, u32[]{:S(2)}, u32[]{:S(2)}) collective-permute-start(f32[2,4,1,128]{3,2,1,0:T(1,128)S(1)} %get-tuple-element.17), channel_id=1, source_target_pairs={{0,1},{2,3},{4,5},{6,7},{8,9},{10,11},{12,13},{14,15},{16,17},{18,... | collective-permute-start | bytes 12296 | tf_op jit(solution)/shard_map/ppermute | solution.py:22
  15.5 5.4 %collective-permute-start.4 = (f32[2,1,64,128]{3,2,1,0:T(8,128)S(1)}, f32[2,1,64,128]{3,2,1,0:T(8,128)S(1)}, u32[]{:S(2)}, u32[]{:S(2)}) collective-permute-start(f32[2,1,64,128]{3,2,1,0:T(8,128)S(1)} %get-tuple-element.23), channel_id=1, source_target_pairs={{2,0},{4,2},{6,4},{8,6},{10,8},{12,10},{14,12},{16,14},{18,16},{20... | collective-permute-start | bytes 196616 | tf_op jit(solution)/shard_map/ppermute | solution.py:24
  16.8 5.0 %collective-permute-start.5 = (f32[2,1,64,128]{3,2,1,0:T(8,128)S(1)}, f32[2,1,64,128]{3,2,1,0:T(8,128)S(1)}, u32[]{:S(2)}, u32[]{:S(2)}) collective-permute-start(f32[2,1,64,128]{3,2,1,0:T(8,128)S(1)} %get-tuple-element.22), channel_id=1, source_target_pairs={{0,2},{2,4},{4,6},{6,8},{8,10},{10,12},{12,14},{14,16},{16,18},{18... | collective-permute-start | bytes 196616 | tf_op jit(solution)/shard_map/ppermute | solution.py:22
  21.8 5.8 %collective-permute-start.6 = (f32[2,4,1,128]{3,2,1,0:T(1,128)S(1)}, f32[2,4,1,128]{3,2,1,0:T(1,128)S(1)}, u32[]{:S(2)}, u32[]{:S(2)}) collective-permute-start(f32[2,4,1,128]{3,2,1,0:T(1,128)S(1)} %get-tuple-element.14), channel_id=1, source_target_pairs={{1,0},{3,2},{5,4},{7,6},{9,8},{11,10},{13,12},{15,14},{17,16},{19,... | collective-permute-start | bytes 12296 | tf_op jit(solution)/shard_map/ppermute | solution.py:24
  23.1 5.9 %collective-permute-start.7 = (f32[2,4,1,128]{3,2,1,0:T(1,128)S(1)}, f32[2,4,1,128]{3,2,1,0:T(1,128)S(1)}, u32[]{:S(2)}, u32[]{:S(2)}) collective-permute-start(f32[2,4,1,128]{3,2,1,0:T(1,128)S(1)} %get-tuple-element.15), channel_id=1, source_target_pairs={{0,1},{2,3},{4,5},{6,7},{8,9},{10,11},{12,13},{14,15},{16,17},{18,... | collective-permute-start | bytes 12296 | tf_op jit(solution)/shard_map/ppermute | solution.py:22
  29.2 7.1 %collective-permute-start.8 = (f32[2,1,64,128]{3,2,1,0:T(8,128)S(1)}, f32[2,1,64,128]{3,2,1,0:T(8,128)S(1)}, u32[]{:S(2)}, u32[]{:S(2)}) collective-permute-start(f32[2,1,64,128]{3,2,1,0:T(8,128)S(1)} %get-tuple-element.21), channel_id=1, source_target_pairs={{2,0},{4,2},{6,4},{8,6},{10,8},{12,10},{14,12},{16,14},{18,16},{20... | collective-permute-start | bytes 196616 | tf_op jit(solution)/shard_map/ppermute | solution.py:24
  30.5 6.7 %collective-permute-start.9 = (f32[2,1,64,128]{3,2,1,0:T(8,128)S(1)}, f32[2,1,64,128]{3,2,1,0:T(8,128)S(1)}, u32[]{:S(2)}, u32[]{:S(2)}) collective-permute-start(f32[2,1,64,128]{3,2,1,0:T(8,128)S(1)} %get-tuple-element.20), channel_id=1, source_target_pairs={{0,2},{2,4},{4,6},{6,8},{8,10},{10,12},{12,14},{14,16},{16,18},{18... | collective-permute-start | bytes 196616 | tf_op jit(solution)/shard_map/ppermute | solution.py:22
  37.2 5.9 %collective-permute-start.10 = (f32[2,4,1,128]{3,2,1,0:T(1,128)S(1)}, f32[2,4,1,128]{3,2,1,0:T(1,128)S(1)}, u32[]{:S(2)}, u32[]{:S(2)}) collective-permute-start(f32[2,4,1,128]{3,2,1,0:T(1,128)S(1)} %get-tuple-element.12), channel_id=1, source_target_pairs={{1,0},{3,2},{5,4},{7,6},{9,8},{11,10},{13,12},{15,14},{17,16},{19,... | collective-permute-start | bytes 12296 | tf_op jit(solution)/shard_map/ppermute | solution.py:24
  38.5 5.9 %collective-permute-start.11 = (f32[2,4,1,128]{3,2,1,0:T(1,128)S(1)}, f32[2,4,1,128]{3,2,1,0:T(1,128)S(1)}, u32[]{:S(2)}, u32[]{:S(2)}) collective-permute-start(f32[2,4,1,128]{3,2,1,0:T(1,128)S(1)} %get-tuple-element.13), channel_id=1, source_target_pairs={{0,1},{2,3},{4,5},{6,7},{8,9},{10,11},{12,13},{14,15},{16,17},{18,... | collective-permute-start | bytes 12296 | tf_op jit(solution)/shard_map/ppermute | solution.py:22
  44.5 7.4 %collective-permute-start.12 = (f32[2,1,64,128]{3,2,1,0:T(8,128)S(1)}, f32[2,1,64,128]{3,2,1,0:T(8,128)S(1)}, u32[]{:S(2)}, u32[]{:S(2)}) collective-permute-start(f32[2,1,64,128]{3,2,1,0:T(8,128)S(1)} %get-tuple-element.19), channel_id=1, source_target_pairs={{2,0},{4,2},{6,4},{8,6},{10,8},{12,10},{14,12},{16,14},{18,16},{20... | collective-permute-start | bytes 196616 | tf_op jit(solution)/shard_map/ppermute | solution.py:24
  45.8 6.9 %collective-permute-start.13 = (f32[2,1,64,128]{3,2,1,0:T(8,128)S(1)}, f32[2,1,64,128]{3,2,1,0:T(8,128)S(1)}, u32[]{:S(2)}, u32[]{:S(2)}) collective-permute-start(f32[2,1,64,128]{3,2,1,0:T(8,128)S(1)} %get-tuple-element.18), channel_id=1, source_target_pairs={{0,2},{2,4},{4,6},{6,8},{8,10},{10,12},{12,14},{14,16},{16,18},{18... | collective-permute-start | bytes 196616 | tf_op jit(solution)/shard_map/ppermute | solution.py:22
  52.7 5.9 %collective-permute-start.14 = (f32[2,4,1,128]{3,2,1,0:T(1,128)S(1)}, f32[2,4,1,128]{3,2,1,0:T(1,128)S(1)}, u32[]{:S(2)}, u32[]{:S(2)}) collective-permute-start(f32[2,4,1,128]{3,2,1,0:T(1,128)S(1)} %get-tuple-element.10), channel_id=1, source_target_pairs={{1,0},{3,2},{5,4},{7,6},{9,8},{11,10},{13,12},{15,14},{17,16},{19,... | collective-permute-start | bytes 12296 | tf_op jit(solution)/shard_map/ppermute | solution.py:24
  54.0 5.9 %collective-permute-start.15 = (f32[2,4,1,128]{3,2,1,0:T(1,128)S(1)}, f32[2,4,1,128]{3,2,1,0:T(1,128)S(1)}, u32[]{:S(2)}, u32[]{:S(2)}) collective-permute-start(f32[2,4,1,128]{3,2,1,0:T(1,128)S(1)} %get-tuple-element.11), channel_id=1, source_target_pairs={{0,1},{2,3},{4,5},{6,7},{8,9},{10,11},{12,13},{14,15},{16,17},{18,... | collective-permute-start | bytes 12296 | tf_op jit(solution)/shard_map/ppermute | solution.py:22
  62.3 7.3 %all-to-all-start = ((f32[2,1,512]{2,1,0:T(1,128)}), f32[2,1,512]{2,1,0:T(1,128)S(1)}, u32[]{:S(2)}, u32[]{:S(2)}) async-start(f32[2,1,512]{2,1,0:T(1,128)} %reshape.169), calls=%async_computation | async-start | bytes 8192 | tf_op jit(solution)/shard_map/all_to_all | solution.py:81
